TPU v7x, 256 devices: a whole 4x4x8 slice. The times are simulated.
256 devices in a mesh: out: 16 (over y, x), inp: 16 (over z, core).
Axes of the slice: x: 4, y: 4, z: 8, core: 2. Of those that a mesh axis runs over, the one named last changes fastest.
Arguments:
- grads: bfloat16 [2048, 28672], P('out', 'inp'), may hold values from -1.1953125 to 1.1953125
- acts: bfloat16 [2048, 8192], P('inp', 'out'), may hold values from -6 to 6
- basis_out: bfloat16 [28672, 14336], P('inp', 'out'), may hold values from -0.03125 to 0.03125
- basis_in: bfloat16 [8192, 8192], P('out', 'inp'), may hold values from -0.0625 to 0.0625
- old_correction: float32 [14336, 8192], P('out', 'inp'), may hold values from 0.1 to 2
- lengths: int32 [16], replicated, may hold values from 1 to 256, 2048 in all
Outputs:
- correction: float32 [14336, 8192], P('out', 'inp')
Inputs may be any that keep to these rules, and one draw needn't show every extreme that they name: The lengths sum to 2048; the longest example has exactly 256 tokens.
All inputs are finite; a program needn't handle non-finite values.
Results may differ from a plain program's by a relative error of at most 0.0021.
Values may be sent and summed in bfloat16 or wider, within the bound.
No kernel may reach another device: no remote copies, remote signals or barrier semaphores. Data moves between devices by JAX's collectives and lax.ppermute only.
A program may use at most 128 MiB of HBM per device.

v0:
```python
import jax
import jax.numpy as jnp
from jax import lax
from jax.sharding import PartitionSpec as P

CAP = 256


def body(grads, acts, basis_out, basis_in, old_correction, lengths):
    gathered = lax.all_gather(grads, "out", axis=0, tiled=True)
    row_count = gathered.shape[0]
    scattered = lax.psum_scatter(
        lax.dot_general(
            basis_out, gathered, (((0,), (1,)), ((), ())), preferred_element_type=jnp.float32
        ),
        "inp",
        scatter_dimension=0,
        tiled=True,
    )
    grad_rot = lax.all_gather(scattered.astype(jnp.bfloat16), "inp", axis=0, tiled=True)
    token_dim = 1
    gathered_acts = lax.all_gather(acts, "inp", axis=0, tiled=True)
    act_scattered = lax.psum_scatter(
        jnp.dot(gathered_acts, basis_in, preferred_element_type=jnp.float32),
        "out",
        scatter_dimension=0,
        tiled=True,
    )
    act_rot = lax.all_gather(act_scattered.astype(jnp.bfloat16), "out", axis=0, tiled=True)
    offsets = jnp.cumsum(lengths) - lengths
    examples = lengths.shape[0]

    def add_example(example, running):
        offset = offsets[example]
        length = lengths[example]
        first_row = jnp.minimum(offset, row_count - CAP)
        places = first_row + jnp.arange(CAP, dtype=jnp.int32)
        inside = (places >= offset) & (places < offset + length)
        grad_block = lax.dynamic_slice_in_dim(grad_rot, first_row, CAP, token_dim)
        act_block = lax.dynamic_slice_in_dim(act_rot, first_row, CAP, 0)
        act_block = jnp.where(inside[:, None], act_block, jnp.zeros((), act_block.dtype))
        projected = lax.dot_general(
            grad_block,
            act_block,
            (((token_dim,), (0,)), ((), ())),
            preferred_element_type=jnp.float32,
        )
        return running + projected * projected

    running = lax.fori_loop(0, examples, add_example, jnp.zeros(old_correction.shape, jnp.float32))
    return 0.8 * old_correction + 0.2 * running / examples


def solution(mesh):
    in_specs = (
        P("out", "inp"),
        P("inp", "out"),
        P("inp", "out"),
        P("out", "inp"),
        P("out", "inp"),
        P(),
    )
    out_specs = P("out", "inp")
    return jax.shard_map(body, mesh=mesh, in_specs=in_specs, out_specs=out_specs, check_vma=False)
```

profile of v0, /device:TPU:1, one launch (start us, length us, event | category | flops | bytes accessed | tf_op | source)
XLA Modules:
  0.0 505.1 jit_solution(16237639878966446037)
XLA Ops:
  6.5 0.7 all-gather.9.cloned.1.call-update
  7.3 0.7 all-gather.5.cloned.1.call-update
  8.1 45.1 %all-gather.9.cloned.1.call-done = bf16[2048,512]{1,0:T(8,128)(2,1)} async-done(((bf16[128,512]{1,0:T(8,128)(2,1)}), bf16[2048,512]{1,0:T(8,128)(2,1)}) %all-gather.9.cloned.1.call-update) | async-done | bytes 2097168 | tf_op jit(solution)/shard_map/all_gather | solution.py:22
  53.2 4.9 fusion.8
  58.1 66.5 %all-gather.5.cloned.1.call-done = bf16[2048,1792]{1,0:T(8,128)(2,1)} async-done(((bf16[128,1792]{1,0:T(8,128)(2,1)}), bf16[2048,1792]{1,0:T(8,128)(2,1)}) %all-gather.5.cloned.1.call-update) | async-done | bytes 7340048 | tf_op jit(solution)/shard_map/all_gather | solution.py:10
  124.7 10.9 %fusion.7 = f32[896,2048]{1,0:T(8,128)} fusion(bf16[1792,896]{1,0:T(8,128)(2,1)S(1)} %copy-done, bf16[2048,1792]{1,0:T(8,128)(2,1)} %all-gather.5.cloned.1.call-done), kind=kOutput, calls=%fused_computation.10 | convolution fusion | flops 6576668672 | bytes 17891328 | tf_op jit(solution)/shard_map/dot_general | solution.py:13
  135.7 73.4 %reduce-scatter.5.cloned.1.call-done = f32[128,512]{1,0:T(8,128)} async-done(((f32[2048,512]{1,0:T(8,128)}), f32[128,512]{1,0:T(8,128)}) %reduce-scatter.5.cloned.1.call-update) | async-done | bytes 262160 | tf_op jit(solution)/shard_map/reduce_scatter | solution.py:23
  209.1 1.6 convert_element_type.7
  210.8 67.7 %reduce-scatter.3.cloned.1.call-done = f32[56,2048]{1,0:T(8,128)} async-done(((f32[896,2048]{1,0:T(8,128)}), f32[56,2048]{1,0:T(8,128)}) %reduce-scatter.3.cloned.1.call-update) | async-done | bytes 458768 | tf_op jit(solution)/shard_map/reduce_scatter | solution.py:12
  278.4 1.7 convert_element_type.6
  280.5 51.2 %all-gather.11.cloned.1.call-done = bf16[2048,512]{1,0:T(8,128)(2,1)} async-done(((bf16[128,512]{1,0:T(8,128)(2,1)}), bf16[2048,512]{1,0:T(8,128)(2,1)}) %all-gather.11.cloned.1.call-update) | async-done | bytes 2097168 | tf_op jit(solution)/shard_map/all_gather | solution.py:29
  331.6 44.1 %all-gather.7.cloned.1.call-done = bf16[896,2048]{1,0:T(8,128)(2,1)} async-done(((bf16[56,2048]{1,0:T(8,128)(2,1)}), bf16[896,2048]{1,0:T(8,128)(2,1)}) %all-gather.7.cloned.1.call-update) | async-done | bytes 3670032 | tf_op jit(solution)/shard_map/all_gather | solution.py:20
  375.7 118.8 %while.14 = (s32[]{:T(128)}, f32[896,512]{1,0:T(8,128)}, s32[16]{0:T(128)S(1)}, bf16[896,2048]{1,0:T(8,128)(2,1)}, s32[16]{0:T(128)S(1)}, /*index=5*/bf16[2048,5...) while((s32[]{:T(128)}, f32[896,512]{1,0:T(8,128)}, s32[16]{0:T(128)S(1)}, ...), condition=%wide.region_4.5_spmd.clone, body=%wide.region_3.4_spmd.clone.sunk | while | flops 236389376 | bytes 4393164 | solution.py:50
  375.7 0.7 dynamic_slice.44
  377.1 0.6 dynamic_slice.45
  379.0 0.7 compare_and_fusion.2
  379.7 2.9 select_add_fusion.2
  382.6 0.7 dynamic_slice.44
  384.0 0.6 dynamic_slice.45
  385.8 0.7 compare_and_fusion.2
  386.5 3.5 select_add_fusion.2
  390.1 0.7 dynamic_slice.44
  393.3 0.7 compare_and_fusion.2
  394.0 3.5 select_add_fusion.2
  397.5 0.7 dynamic_slice.44
  400.8 0.7 compare_and_fusion.2
  401.5 3.5 select_add_fusion.2
  405.0 0.7 dynamic_slice.44
  408.2 0.7 compare_and_fusion.2
  408.9 3.5 select_add_fusion.2
  412.5 0.7 dynamic_slice.44
  415.7 0.7 compare_and_fusion.2
  416.4 3.5 select_add_fusion.2
  420.0 0.7 dynamic_slice.44
  423.2 0.7 compare_and_fusion.2
  423.9 3.5 select_add_fusion.2
  427.5 0.7 dynamic_slice.44
  430.7 0.7 compare_and_fusion.2
  431.4 3.5 select_add_fusion.2
  434.9 0.7 dynamic_slice.44
  438.2 0.7 compare_and_fusion.2
  438.9 3.5 select_add_fusion.2
  442.4 0.7 dynamic_slice.44
  445.6 0.7 compare_and_fusion.2
  446.3 3.5 select_add_fusion.2
  449.9 0.7 dynamic_slice.44
  453.1 0.7 compare_and_fusion.2
  453.8 3.5 select_add_fusion.2
  457.4 0.7 dynamic_slice.44
  460.6 0.7 compare_and_fusion.2
  461.3 3.5 select_add_fusion.2
  464.8 0.7 dynamic_slice.44
  468.1 0.7 compare_and_fusion.2
  468.8 3.5 select_add_fusion.2
  472.3 0.7 dynamic_slice.44
  475.5 0.7 compare_and_fusion.2
  476.3 3.5 select_add_fusion.2
  479.7 0.7 dynamic_slice.44
  483.0 0.7 compare_and_fusion.2
  483.7 3.5 select_add_fusion.2
  487.1 0.7 dynamic_slice.44
  490.4 0.7 compare_and_fusion.2
  491.1 3.5 select_add_fusion.2
  494.6 3.7 multiply_add_fusion
  (33 shorter events, 8.9 us)
Async XLA Ops:
  6.5 118.1 %copy-start = (bf16[1792,896]{1,0:T(8,128)(2,1)S(1)}, bf16[1792,896]{1,0:T(8,128)(2,1)}, u32[]{:S(2)}) copy-start(bf16[1792,896]{1,0:T(8,128)(2,1)} %param.10) | copy-start | bytes 9633796
  6.5 46.6 %all-gather.9.cloned.1.call-start = ((), (), s32[]{:S(2)}) async-start(), calls=%async_computation.5 | async-start | bytes 2228224 | tf_op jit(solution)/shard_map/all_gather | solution.py:22
  7.3 117.4 %all-gather.5.cloned.1.call-start = ((), (), s32[]{:S(2)}) async-start(), calls=%async_computation.2 | async-start | bytes 7798784 | tf_op jit(solution)/shard_map/all_gather | solution.py:10
  8.0 201.1 %reduce-scatter.5.cloned.1.call-start = ((), (), s32[]{:S(2)}) async-start(), calls=%async_computation.6 | async-start | bytes 4456448 | tf_op jit(solution)/shard_map/reduce_scatter | solution.py:23
  58.1 220.3 %reduce-scatter.3.cloned.1.call-start = ((), (), s32[]{:S(2)}) async-start(), calls=%async_computation.3 | async-start | bytes 7798784 | tf_op jit(solution)/shard_map/reduce_scatter | solution.py:12
  135.6 144.6 %copy-start.1 = (s32[16]{0:T(128)S(1)}, s32[16]{0:T(128)}, u32[]{:S(2)}) copy-start(s32[16]{0:T(128)} %param.13) | copy-start | bytes 196
  135.6 196.0 %all-gather.11.cloned.1.call-start = ((), (), s32[]{:S(2)}) async-start(), calls=%async_computation.7 | async-start | bytes 2228224 | tf_op jit(solution)/shard_map/all_gather | solution.py:29
  210.7 165.0 %all-gather.7.cloned.1.call-start = ((), (), s32[]{:S(2)}) async-start(), calls=%async_computation.4 | async-start | bytes 3899392 | tf_op jit(solution)/shard_map/all_gather | solution.py:20
Sparse Core Ops, SparseCore 0:
  9.2 43.9 all-gather.8
  55.6 69.0 all-gather.4
  128.3 80.7 reduce-scatter.4
  211.7 66.7 reduce-scatter.2
  281.0 50.5 all-gather.10
  333.5 42.2 all-gather.6
where the time goes:
time: 506 us; the launch traced here: 505 us
  waiting for transfers between devices  349 us (69%)
  matrix products  71.7 us (14%)
  loops' own time  31.7 us (6%)
  local copies, waits for them, and re-layouts  20.2 us (4%)
  other arithmetic  18.3 us (4%)
  between operations  13.5 us (3%)
    reduce_scatter x1, waiting for transfers between devices, body(): lax.psum_scatter(jnp.dot(gathered_acts, basis_in, preferred_element_type=...  73.4 us
    reduce_scatter x1, waiting for transfers between devices, body(): lax.psum_scatter(lax.dot_general(basis_out, gathered, (((0,), (1,)), ((),...  67.7 us
    all_gather x1, waiting for transfers between devices, body(): gathered = lax.all_gather(grads, 'out', axis=0, tiled=True)  66.5 us
    dot_general x16, matrix products, add_example(): lax.dot_general(grad_block, act_block, (((token_dim,), (0,)), ((), ())),...  55.9 us
    all_gather x1, waiting for transfers between devices, body(): lax.all_gather(act_scattered.astype(jnp.bfloat16), 'out', axis=0, tiled=T...  51.2 us
    all_gather x1, waiting for transfers between devices, body(): gathered_acts = lax.all_gather(acts, 'inp', axis=0, tiled=True)  45.1 us
    all_gather x1, waiting for transfers between devices, body(): lax.all_gather(scattered.astype(jnp.bfloat16), 'inp', axis=0, tiled=True)  44.1 us
    another operation x1, loops' own time, body(): lax.fori_loop(0, examples, add_example, jnp.zeros(old_correction.shape, j...  31.7 us
  transfers between devices with their start and end apart: 6, of which 6 were waited for; matrix products, arithmetic and copies ran while one was open for 4% of the time, Pallas kernels for 0%

commit v1 on v0

--- a/solution.py
+++ b/solution.py
@@ -7,7 +7,9 @@
 
 
 def body(grads, acts, basis_out, basis_in, old_correction, lengths):
-    gathered = lax.all_gather(grads, "out", axis=0, tiled=True)
+    gathered = jnp.concatenate(
+        lax.all_to_all(jnp.stack([grads] * lax.axis_size("out")), "out", 0, 0), axis=0
+    )
     row_count = gathered.shape[0]
     scattered = lax.psum_scatter(
         lax.dot_general(

time: 506 us -> 480 us (0.949)
  waiting for transfers between devices: 349 us -> 312 us
  starting transfers between devices: 0.2 us -> 7.8 us
    all_to_all x0 -> x1, waiting for transfers between devices: none -> 74.7 us  [body(): lax.all_to_all(jnp.stack([grads] * lax.axis_size('out')), 'out', 0, 0)]
    all_gather x1 -> x0, waiting for transfers between devices: 66.5 us -> none  [body(): gathered = lax.all_gather(grads, 'out', axis=0, tiled=True)]
    reduce_scatter x1, waiting for transfers between devices: 73.4 us -> 40.2 us  [body(): lax.psum_scatter(jnp.dot(gathered_acts, basis_in, preferred_element_type=...]
    all_gather x1, waiting for transfers between devices: 45.1 us -> 33.1 us  [body(): gathered_acts = lax.all_gather(acts, 'inp', axis=0, tiled=True)]
    all_to_all x0 -> x1, starting transfers between devices: none -> 7.63 us  [body(): lax.all_to_all(jnp.stack([grads] * lax.axis_size('out')), 'out', 0, 0)]
  transfers between devices with their start and end apart: 6 -> 6, of which waited for: 6 -> 6; matrix products, arithmetic and copies ran while one was open for 4% -> 5% of each run, Pallas kernels for 0% -> 0%
where the time goes in v1:
time: 480 us; the launch traced here: 478 us
  waiting for transfers between devices  312 us (65%)
  matrix products  71.9 us (15%)
  loops' own time  31.2 us (6%)
  local copies, waits for them, and re-layouts  25.2 us (5%)
  other arithmetic  17.1 us (4%)
  between operations  13.2 us (3%)
  starting transfers between devices  7.8 us (2%)
    all_to_all x1, waiting for transfers between devices, body(): lax.all_to_all(jnp.stack([grads] * lax.axis_size('out')), 'out', 0, 0)  74.7 us
    reduce_scatter x1, waiting for transfers between devices, body(): lax.psum_scatter(lax.dot_general(basis_out, gathered, (((0,), (1,)), ((),...  67.7 us
    dot_general x16, matrix products, add_example(): lax.dot_general(grad_block, act_block, (((token_dim,), (0,)), ((), ())),...  55.9 us
    all_gather x1, waiting for transfers between devices, body(): lax.all_gather(act_scattered.astype(jnp.bfloat16), 'out', axis=0, tiled=T...  51.4 us
    all_gather x1, waiting for transfers between devices, body(): lax.all_gather(scattered.astype(jnp.bfloat16), 'inp', axis=0, tiled=True)  44.1 us
    reduce_scatter x1, waiting for transfers between devices, body(): lax.psum_scatter(jnp.dot(gathered_acts, basis_in, preferred_element_type=...  40.2 us
    all_gather x1, waiting for transfers between devices, body(): gathered_acts = lax.all_gather(acts, 'inp', axis=0, tiled=True)  33.1 us
    another operation x1, loops' own time, body(): lax.fori_loop(0, examples, add_example, jnp.zeros(old_correction.shape, j...  31.2 us
  transfers between devices with their start and end apart: 6, of which 6 were waited for; matrix products, arithmetic and copies ran while one was open for 5% of the time, Pallas kernels for 0%

profile of v1, /device:TPU:1, one launch (start us, length us, event | category | flops | bytes accessed | tf_op | source)
XLA Modules:
  0.0 478.3 jit_solution(12800500948629236278)
XLA Ops:
  6.5 0.7 all-gather.6.cloned.1.call-update
  7.3 4.9 %stack.2 = bf16[16,128,1792]{2,1,0:T(8,128)(2,1)} broadcast(bf16[128,1792]{1,0:T(8,128)(2,1)} %param.8), dimensions={1,2} | broadcast | bytes 7798784 | tf_op jit(solution)/shard_map/stack | solution.py:11
  12.2 7.6 %all-to-all-start = ((bf16[16,128,1792]{2,1,0:T(8,128)(2,1)}), bf16[16,128,1792]{2,1,0:T(8,128)(2,1)}, u32[]{:S(2)}, u32[]{:S(2)}) async-start(bf16[16,128,1792]{2,1,0:T(8,128)(2,1)} %stack.2), calls=%async_computation | async-start | bytes 14680064 | tf_op jit(solution)/shard_map/all_to_all | solution.py:11
  19.9 33.1 %all-gather.6.cloned.1.call-done = bf16[2048,512]{1,0:T(8,128)(2,1)} async-done(((bf16[128,512]{1,0:T(8,128)(2,1)}), bf16[2048,512]{1,0:T(8,128)(2,1)}) %all-gather.6.cloned.1.call-update) | async-done | bytes 2097168 | tf_op jit(solution)/shard_map/all_gather | solution.py:24
  53.0 4.9 %fusion.8 = f32[2048,512]{1,0:T(8,128)} fusion(bf16[2048,512]{1,0:T(8,128)(2,1)} %all-gather.6.cloned.1.call-done, bf16[512,512]{1,0:T(8,128)(2,1)} %param.11), kind=kOutput, calls=%fused_computation.11 | convolution fusion | flops 1073741824 | bytes 6815744 | tf_op jit(solution)/shard_map/dot_general | solution.py:26
  58.0 74.7 %all-to-all-done = bf16[16,128,1792]{2,1,0:T(8,128)(2,1)} async-done(((bf16[16,128,1792]{2,1,0:T(8,128)(2,1)}), bf16[16,128,1792]{2,1,0:T(8,128)(2,1)}, u32[]{:S(2)}, u32[]{:S(2)}) %all-to-all-start) | async-done | bytes 7340064 | tf_op jit(solution)/shard_map/all_to_all | solution.py:11
  132.7 11.1 %fusion.7 = f32[896,2048]{1,0:T(8,128)} fusion(bf16[1792,896]{1,0:T(8,128)(2,1)S(1)} %copy-done, bf16[2048,1792]{1,0:T(8,128)(2,1)} %bitcast.1), kind=kOutput, calls=%fused_computation.10 | convolution fusion | flops 6576668672 | bytes 17891328 | tf_op jit(solution)/shard_map/dot_general | solution.py:15
  143.9 40.2 %reduce-scatter.5.cloned.1.call-done = f32[128,512]{1,0:T(8,128)} async-done(((f32[2048,512]{1,0:T(8,128)}), f32[128,512]{1,0:T(8,128)}) %reduce-scatter.5.cloned.1.call-update) | async-done | bytes 262160 | tf_op jit(solution)/shard_map/reduce_scatter | solution.py:25
  184.1 1.6 convert_element_type.7
  185.8 67.7 %reduce-scatter.3.cloned.1.call-done = f32[56,2048]{1,0:T(8,128)} async-done(((f32[896,2048]{1,0:T(8,128)}), f32[56,2048]{1,0:T(8,128)}) %reduce-scatter.3.cloned.1.call-update) | async-done | bytes 458768 | tf_op jit(solution)/shard_map/reduce_scatter | solution.py:14
  253.5 1.7 convert_element_type.6
  255.5 51.4 %all-gather.8.cloned.1.call-done = bf16[2048,512]{1,0:T(8,128)(2,1)} async-done(((bf16[128,512]{1,0:T(8,128)(2,1)}), bf16[2048,512]{1,0:T(8,128)(2,1)}) %all-gather.8.cloned.1.call-update) | async-done | bytes 2097168 | tf_op jit(solution)/shard_map/all_gather | solution.py:31
  306.8 44.1 %all-gather.4.cloned.1.call-done = bf16[896,2048]{1,0:T(8,128)(2,1)} async-done(((bf16[56,2048]{1,0:T(8,128)(2,1)}), bf16[896,2048]{1,0:T(8,128)(2,1)}) %all-gather.4.cloned.1.call-update) | async-done | bytes 3670032 | tf_op jit(solution)/shard_map/all_gather | solution.py:22
  350.9 117.1 %while.14 = (s32[]{:T(128)}, f32[896,512]{1,0:T(8,128)}, s32[16]{0:T(128)S(1)}, bf16[896,2048]{1,0:T(8,128)(2,1)}, s32[16]{0:T(128)S(1)}, /*index=5*/bf16[2048,5...) while((s32[]{:T(128)}, f32[896,512]{1,0:T(8,128)}, s32[16]{0:T(128)S(1)}, ...), condition=%wide.region_4.5_spmd.clone, body=%wide.region_3.4_spmd.clone.sunk | while | flops 236389376 | bytes 4393164 | solution.py:52
  350.9 0.6 dynamic_slice.44
  352.2 0.7 dynamic_slice.45
  354.1 0.6 compare_and_fusion.2
  354.8 2.9 select_add_fusion.2
  358.9 0.7 dynamic_slice.45
  360.9 0.6 compare_and_fusion.2
  361.5 3.5 select_add_fusion.2
  366.3 0.7 dynamic_slice.45
  368.2 0.6 compare_and_fusion.2
  368.9 3.5 select_add_fusion.2
  373.6 0.7 dynamic_slice.45
  375.6 0.6 compare_and_fusion.2
  376.2 3.5 select_add_fusion.2
  381.0 0.7 dynamic_slice.45
  383.0 0.6 compare_and_fusion.2
  383.6 3.5 select_add_fusion.2
  388.4 0.7 dynamic_slice.45
  390.4 0.6 compare_and_fusion.2
  391.0 3.5 select_add_fusion.2
  395.7 0.7 dynamic_slice.45
  397.7 0.6 compare_and_fusion.2
  398.4 3.5 select_add_fusion.2
  403.1 0.7 dynamic_slice.45
  405.1 0.6 compare_and_fusion.2
  405.7 3.5 select_add_fusion.2
  410.5 0.7 dynamic_slice.45
  412.5 0.6 compare_and_fusion.2
  413.1 3.5 select_add_fusion.2
  417.9 0.7 dynamic_slice.45
  419.8 0.6 compare_and_fusion.2
  420.5 3.5 select_add_fusion.2
  425.2 0.7 dynamic_slice.45
  427.2 0.6 compare_and_fusion.2
  427.8 3.5 select_add_fusion.2
  432.6 0.7 dynamic_slice.45
  434.6 0.6 compare_and_fusion.2
  435.2 3.5 select_add_fusion.2
  440.0 0.7 dynamic_slice.45
  441.9 0.6 compare_and_fusion.2
  442.6 3.5 select_add_fusion.2
  447.3 0.7 dynamic_slice.45
  449.3 0.6 compare_and_fusion.2
  449.9 3.5 select_add_fusion.2
  454.6 0.7 dynamic_slice.45
  456.6 0.6 compare_and_fusion.2
  457.2 3.5 select_add_fusion.2
  461.9 0.7 dynamic_slice.45
  463.9 0.6 compare_and_fusion.2
  464.5 3.5 select_add_fusion.2
  468.0 3.7 multiply_add_fusion
  (33 shorter events, 9.3 us)
Async XLA Ops:
  6.5 126.2 %copy-start = (bf16[1792,896]{1,0:T(8,128)(2,1)S(1)}, bf16[1792,896]{1,0:T(8,128)(2,1)}, u32[]{:S(2)}) copy-start(bf16[1792,896]{1,0:T(8,128)(2,1)} %param.10) | copy-start | bytes 9633796
  6.5 46.5 %all-gather.6.cloned.1.call-start = ((), (), s32[]{:S(2)}) async-start(), calls=%async_computation.5 | async-start | bytes 2228224 | tf_op jit(solution)/shard_map/all_gather | solution.py:24
  12.2 120.5 %all-to-all-start = ((bf16[16,128,1792]{2,1,0:T(8,128)(2,1)}), bf16[16,128,1792]{2,1,0:T(8,128)(2,1)}, u32[]{:S(2)}, u32[]{:S(2)}) async-start(bf16[16,128,1792]{2,1,0:T(8,128)(2,1)} %stack.2), calls=%async_computation | async-start | bytes 14680064 | tf_op jit(solution)/shard_map/all_to_all | solution.py:11
  19.8 164.3 %reduce-scatter.5.cloned.1.call-start = ((), (), s32[]{:S(2)}) async-start(), calls=%async_computation.6 | async-start | bytes 4456448 | tf_op jit(solution)/shard_map/reduce_scatter | solution.py:25
  57.9 195.5 %reduce-scatter.3.cloned.1.call-start = ((), (), s32[]{:S(2)}) async-start(), calls=%async_computation.3 | async-start | bytes 7798784 | tf_op jit(solution)/shard_map/reduce_scatter | solution.py:14
  143.8 111.4 %copy-start.1 = (s32[16]{0:T(128)S(1)}, s32[16]{0:T(128)}, u32[]{:S(2)}) copy-start(s32[16]{0:T(128)} %param.13) | copy-start | bytes 196
  143.8 163.0 %all-gather.8.cloned.1.call-start = ((), (), s32[]{:S(2)}) async-start(), calls=%async_computation.7 | async-start | bytes 2228224 | tf_op jit(solution)/shard_map/all_gather | solution.py:31
  185.7 165.2 %all-gather.4.cloned.1.call-start = ((), (), s32[]{:S(2)}) async-start(), calls=%async_computation.4 | async-start | bytes 3899392 | tf_op jit(solution)/shard_map/all_gather | solution.py:22
Sparse Core Ops, SparseCore 0:
  9.2 43.7 all-gather.5
  58.1 125.9 reduce-scatter.4
  186.8 66.5 reduce-scatter.2
  256.1 50.7 all-gather.7
  308.7 42.2 all-gather.3
